TPU v7x, 32 devices: a whole 2x2x4 slice. The times are simulated.
32 devices in a mesh: section: 4 (over x, core), seq: 8 (over z, y).
Axes of the slice: x: 2, y: 2, z: 4, core: 2. Of those that a mesh axis runs over, the one named last changes fastest.
Arguments:
- queries: bfloat16 [2048, 512], P('seq', 'section'), may hold values from -64 to 64
- key_rows: bfloat16 [2048, 512], P('seq', 'section'), may hold values from -64 to 64
- values: bfloat16 [2048, 512], P('seq', 'section'), may hold values from -6 to 6
- out_grad: bfloat16 [2048, 512], P('seq', 'section'), may hold values from -6 to 6
- query_gain: float32 [512], P('section'), may hold values from 1 to 3
- key_gain: float32 [512], P('section'), may hold values from 1 to 3
- stretch_id: int32 [2048], P('seq'), may hold values from 0 to 7, as said below
Outputs:
- attended: bfloat16 [2048, 512], P('seq', 'section')
- grad_queries: float32 [2048, 512], P('seq', 'section')
- grad_keys: float32 [2048, 512], P('seq', 'section')
- grad_values: float32 [2048, 512], P('seq', 'section')
Inputs may be any that keep to these rules, and one draw needn't show every extreme that they name: stretch_id never falls along the tokens and changes only at multiples of 128 tokens (whole latent frames); the first frame is stretch 0 alone, stretch 1 spans exactly three frames (384 tokens); from frame 4 on, stretches come in consecutive pairs that together span exactly four frames, each stretch one to three frames.
All inputs are finite; a program needn't handle non-finite values.
Results may differ from a plain program's by a relative error of at most 0.038.
Values may be sent and summed in bfloat16 or wider, within the bound.
A program may use at most 64 MiB of HBM per device.

v0:
```python
import math

import jax
import jax.numpy as jnp
from jax import lax
from jax.sharding import PartitionSpec as P

EPSILON = 1e-06
NEG_FILL = -1e30


def block_length(row_count, shard_rows):
    per_block = max(1, 1024 // shard_rows)
    while row_count % (per_block * shard_rows) != 0:
        per_block = per_block - 1
    return per_block * shard_rows


def in_blocks(shard_piece, shard_rows):
    length = block_length(shard_piece[0].shape[0], shard_rows)
    return jax.tree.map(
        lambda member: member.reshape((member.shape[0] // length, length) + member.shape[1:]),
        shard_piece,
    )


def on_device(queries, key_rows, values, out_grad, query_gain, key_gain, stretch_id):
    shard_rows, head_size = queries.shape
    width = head_size * lax.axis_size("section")
    score_scale = 1.0 / math.sqrt(head_size)
    query_wide = queries.astype(jnp.float32)
    key_wide = key_rows.astype(jnp.float32)
    squares = lax.psum(
        (jnp.sum(query_wide * query_wide, axis=1), jnp.sum(key_wide * key_wide, axis=1)), "section"
    )
    query_root = lax.rsqrt(squares[0] / width + EPSILON)
    key_root = lax.rsqrt(squares[1] / width + EPSILON)
    query_hat = (query_wide * query_root[:, None] * query_gain[None, :]).astype(jnp.bfloat16)
    key_hat = (key_wide * key_root[:, None] * key_gain[None, :]).astype(jnp.bfloat16)

    def forward_block(carried, key_block):
        key_part, value_part, stretch_part = key_block
        accumulated, run_top, run_sum = carried
        scores = (
            jnp.einsum("td,ud->tu", query_hat, key_part, preferred_element_type=jnp.float32)
            * score_scale
        )
        visible = stretch_part[None, :] <= stretch_id[:, None]
        scores = jnp.where(visible, scores, NEG_FILL)
        new_top = jnp.maximum(run_top, jnp.max(scores, axis=1))
        weights = jnp.exp(scores - new_top[:, None])
        factor = jnp.exp(run_top - new_top)
        accumulated = accumulated * factor[:, None] + jnp.dot(
            weights.astype(jnp.bfloat16), value_part, preferred_element_type=jnp.float32
        )
        return ((accumulated, new_top, run_sum * factor + jnp.sum(weights, axis=1)), None)

    zero_rows = jnp.zeros((shard_rows, head_size), jnp.float32)
    initial = (
        zero_rows,
        jnp.full((shard_rows,), NEG_FILL, jnp.float32),
        jnp.zeros((shard_rows,), jnp.float32),
    )
    result, _ = lax.scan(
        forward_block,
        initial,
        in_blocks(
            (
                lax.all_gather(key_hat, "seq", axis=0, tiled=True),
                lax.all_gather(values, "seq", axis=0, tiled=True),
                lax.all_gather(stretch_id, "seq", axis=0, tiled=True),
            ),
            shard_rows,
        ),
    )
    accumulated, run_top, run_sum = result
    attended = (accumulated / run_sum[:, None]).astype(jnp.bfloat16)
    log_total = run_top + jnp.log(run_sum)
    row_delta = jnp.sum(out_grad.astype(jnp.float32) * attended.astype(jnp.float32), axis=1)

    def query_side_update(query_grad, key_block):
        key_part, value_part, stretch_part = key_block
        scores = (
            jnp.einsum("td,ud->tu", query_hat, key_part, preferred_element_type=jnp.float32)
            * score_scale
        )
        visible = stretch_part[None, :] <= stretch_id[:, None]
        chances = jnp.exp(jnp.where(visible, scores, NEG_FILL) - log_total[:, None])
        grad_chances = jnp.einsum(
            "td,ud->tu", out_grad, value_part, preferred_element_type=jnp.float32
        )
        grad_scores = (chances * (grad_chances - row_delta[:, None])).astype(jnp.bfloat16)
        return (
            query_grad
            + jnp.dot(grad_scores, key_part, preferred_element_type=jnp.float32) * score_scale
        )

    def key_side_update(grad_pair, query_block):
        query_part, grad_part, total_part, delta_part, stretch_part = query_block
        key_grad, value_grad = grad_pair
        scores = (
            jnp.einsum("td,ud->tu", query_part, key_hat, preferred_element_type=jnp.float32)
            * score_scale
        )
        visible = stretch_id[None, :] <= stretch_part[:, None]
        chances = jnp.exp(jnp.where(visible, scores, NEG_FILL) - total_part[:, None])
        grad_chances = jnp.einsum(
            "td,ud->tu", grad_part, values, preferred_element_type=jnp.float32
        )
        grad_scores = (chances * (grad_chances - delta_part[:, None])).astype(jnp.bfloat16)
        key_grad = (
            key_grad
            + jnp.einsum("tu,td->ud", grad_scores, query_part, preferred_element_type=jnp.float32)
            * score_scale
        )
        value_grad = value_grad + jnp.einsum(
            "tu,td->ud", chances.astype(jnp.bfloat16), grad_part, preferred_element_type=jnp.float32
        )
        return (key_grad, value_grad)

    def query_step(current, key_block):
        return (query_side_update(current, key_block), None)

    result, _ = lax.scan(
        query_step,
        zero_rows,
        in_blocks(
            (
                lax.all_gather(key_hat, "seq", axis=0, tiled=True),
                lax.all_gather(values, "seq", axis=0, tiled=True),
                lax.all_gather(stretch_id, "seq", axis=0, tiled=True),
            ),
            shard_rows,
        ),
    )
    query_grad = result

    def key_step(current, query_block):
        return (key_side_update(current, query_block), None)

    result, _ = lax.scan(
        key_step,
        (zero_rows, zero_rows),
        in_blocks(
            (
                lax.all_gather(query_hat.astype(jnp.float32), "seq", axis=0, tiled=True).astype(
                    jnp.bfloat16
                ),
                lax.all_gather(out_grad.astype(jnp.float32), "seq", axis=0, tiled=True).astype(
                    jnp.bfloat16
                ),
                lax.all_gather(log_total, "seq", axis=0, tiled=True),
                lax.all_gather(row_delta, "seq", axis=0, tiled=True),
                lax.all_gather(stretch_id, "seq", axis=0, tiled=True),
            ),
            shard_rows,
        ),
    )
    key_grad, value_grad = result
    totals = lax.psum(
        (
            jnp.sum(query_grad * query_gain[None, :] * query_wide, axis=1),
            jnp.sum(key_grad * key_gain[None, :] * key_wide, axis=1),
        ),
        "section",
    )
    grad_queries = (
        query_gain[None, :] * query_root[:, None] * query_grad
        - query_wide * (query_root**3 * totals[0] / width)[:, None]
    )
    grad_keys = (
        key_gain[None, :] * key_root[:, None] * key_grad
        - key_wide * (key_root**3 * totals[1] / width)[:, None]
    )
    return (attended, grad_queries, grad_keys, value_grad)


def solution(mesh):
    placed = (
        P("seq", "section"),
        P("seq", "section"),
        P("seq", "section"),
        P("seq", "section"),
        P("section"),
        P("section"),
        P("seq"),
    )
    return jax.shard_map(
        on_device,
        mesh=mesh,
        in_specs=placed,
        out_specs=(
            P("seq", "section"),
            P("seq", "section"),
            P("seq", "section"),
            P("seq", "section"),
        ),
        check_vma=False,
    )
```

profile of v0, /device:TPU:0, one launch (start us, length us, event | category | flops | bytes accessed | tf_op | source)
XLA Modules:
  0.0 208.2 jit_solution(1747417565312372149)
XLA Ops:
  0.7 22.5 %all-gather = s32[8,1,256]{2,1,0:T(1,128)S(1)} all-gather(s32[1,1,256]{2,1,0:T(1,128)} %bitcast.122), channel_id=1, replica_groups=mesh['section'=4,'seq'=8] {'seq'}, dimensions={0}, use_global_device_ids=true | all-gather | bytes 9216 | tf_op jit(solution)/shard_map/all_gather | solution.py:71
  23.2 1.0 fusion.60
  24.4 5.7 %all-reduce.1 = (f32[256]{0:T(256)S(1)}, f32[256]{0:T(256)S(1)}) all-reduce(f32[256]{0:T(256)S(1)} %fusion.60, f32[256]{0:T(256)S(1)} %fusion.65), channel_id=1, replica_groups=mesh['section'=4,'seq'=8] {'section'}, use_global_device_ids=true, to_apply=%region_1.0 | all-reduce | flops 512 | bytes 4096 | tf_op jit(solution)/shard_map/psum | solution.py:33
  30.1 0.6 copy-done.6
  30.8 31.5 %all_gather.26 = bf16[2048,128]{1,0:T(8,128)(2,1)S(1)} all-gather(bf16[256,128]{1,0:T(8,128)(2,1)S(1)} %fusion.62), channel_id=1, replica_groups=mesh['section'=4,'seq'=8] {'seq'}, dimensions={0}, use_global_device_ids=true | all-gather | bytes 589824 | tf_op jit(solution)/shard_map/all_gather | solution.py:69
  62.3 0.6 copy-done.5
  63.1 0.7 copy-done.2
  63.8 31.4 %all_gather.27 = bf16[2048,128]{1,0:T(8,128)(2,1)S(1)} all-gather(bf16[256,128]{1,0:T(8,128)(2,1)S(1)} %copy-done.2), channel_id=1, replica_groups=mesh['section'=4,'seq'=8] {'seq'}, dimensions={0}, use_global_device_ids=true | all-gather | bytes 589824 | tf_op jit(solution)/shard_map/all_gather | solution.py:70
  95.2 0.7 copy-done.7
  95.9 2.0 while.39
  97.9 0.7 multiply_reduce_fusion
  98.7 1.8 while.40
  99.1 0.5 fusion.116
  100.0 0.5 fusion.116
  100.7 31.2 %all_gather.28 = bf16[2048,128]{1,0:T(8,128)(2,1)S(1)} all-gather(bf16[256,128]{1,0:T(8,128)(2,1)S(1)} %get-tuple-element.651), channel_id=1, replica_groups=mesh['section'=4,'seq'=8] {'seq'}, dimensions={0}, use_global_device_ids=true | all-gather | bytes 589824 | tf_op jit(solution)/shard_map/all_gather | solution.py:146
  131.8 16.5 %all-gather.1 = f32[8,1,256]{2,1,0:T(1,128)S(1)} all-gather(f32[1,1,256]{2,1,0:T(1,128)S(1)} %bitcast.121), channel_id=1, replica_groups=mesh['section'=4,'seq'=8] {'seq'}, dimensions={0}, use_global_device_ids=true | all-gather | bytes 9216 | tf_op jit(solution)/shard_map/all_gather | solution.py:152
  148.4 31.2 %all_gather.30 = bf16[2048,128]{1,0:T(8,128)(2,1)S(1)} all-gather(bf16[256,128]{1,0:T(8,128)(2,1)S(1)} %get-tuple-element.647), channel_id=1, replica_groups=mesh['section'=4,'seq'=8] {'seq'}, dimensions={0}, use_global_device_ids=true | all-gather | bytes 589824 | tf_op jit(solution)/shard_map/all_gather | solution.py:149
  179.6 18.0 %all-gather.2 = f32[8,1,256]{2,1,0:T(1,128)S(1)} all-gather(f32[1,1,256]{2,1,0:T(1,128)S(1)} %bitcast.120), channel_id=1, replica_groups=mesh['section'=4,'seq'=8] {'seq'}, dimensions={0}, use_global_device_ids=true | all-gather | bytes 9216 | tf_op jit(solution)/shard_map/all_gather | solution.py:153
  197.7 3.1 %while.41 = (s32[]{:T(128)}, f32[256,128]{1,0:T(8,128)S(1)}, f32[256,128]{1,0:T(8,128)S(1)}, s32[256]{0:T(256)S(1)}, s32[2,1024]{1,0:T(2,128)S(1)}, /*index=5*/b...) while((s32[]{:T(128)}, f32[256,128]{1,0:T(8,128)S(1)}, ...), condition=%wide.region_14.15_spmd.clone, body=%wide.region_13.14_spmd.clone.sunk | while | flops 270696448 | bytes 4889247 | solution.py:141
  198.2 0.7 fusion.125
  199.7 0.7 fusion.125
  200.9 5.7 %all-reduce = (f32[256]{0:T(256)S(1)}, f32[256]{0:T(256)S(1)}) all-reduce(f32[256]{0:T(256)S(1)} %fusion.68, f32[256]{0:T(256)S(1)} %fusion.63), channel_id=1, replica_groups=mesh['section'=4,'seq'=8] {'section'}, use_global_device_ids=true, to_apply=%region_12.13 | all-reduce | flops 512 | bytes 4096 | tf_op jit(solution)/shard_map/psum | solution.py:160
  206.6 0.8 fusion.69
  207.4 0.8 fusion.64
  (59 shorter events, 5.1 us)
Async XLA Ops:
  0.6 23.6 %copy-start.3 = (bf16[256,128]{1,0:T(8,128)(2,1)S(1)}, bf16[256,128]{1,0:T(8,128)(2,1)}, u32[]{:S(2)}) copy-start(bf16[256,128]{1,0:T(8,128)(2,1)} %param.13) | copy-start | bytes 196612
  23.2 6.8 %copy-start.4 = (bf16[256,128]{1,0:T(8,128)(2,1)S(1)}, bf16[256,128]{1,0:T(8,128)(2,1)}, u32[]{:S(2)}) copy-start(bf16[256,128]{1,0:T(8,128)(2,1)} %param.14) | copy-start | bytes 196612
  30.0 0.7 copy-start.6
  62.3 0.7 copy-start.5
  63.0 0.8 copy-start.2
  95.2 0.7 copy-start.7
  95.9 2.1 copy-start.1
  200.8 6.6 %copy-start = (f32[256,128]{1,0:T(8,128)}, f32[256,128]{1,0:T(8,128)S(1)}, u32[]{:S(2)}) copy-start(f32[256,128]{1,0:T(8,128)S(1)} %get-tuple-element.162) | copy-start | bytes 393220
where the time goes:
time: 209 us; the launch traced here: 208 us
  blocking collectives  194 us (93%)
  matrix products  6.14 us (3%)
  other arithmetic  4.48 us (2%)
  local copies, waits for them, and re-layouts  2.85 us (1%)
    all_gather x1, blocking collectives, on_device(): lax.all_gather(key_hat, 'seq', axis=0, tiled=True)  31.5 us
    all_gather x1, blocking collectives, on_device(): lax.all_gather(values, 'seq', axis=0, tiled=True)  31.4 us
    all_gather x1, blocking collectives, on_device(): lax.all_gather(out_grad.astype(jnp.float32), 'seq', axis=0, tiled=True)  31.2 us
    all_gather x1, blocking collectives, on_device(): lax.all_gather(query_hat.astype(jnp.float32), 'seq', axis=0, tiled=True)  31.2 us
    all_gather x1, blocking collectives, on_device(): lax.all_gather(stretch_id, 'seq', axis=0, tiled=True)  22.5 us
    all_gather x1, blocking collectives, on_device(): lax.all_gather(row_delta, 'seq', axis=0, tiled=True)  18 us
    all_gather x1, blocking collectives, on_device(): lax.all_gather(log_total, 'seq', axis=0, tiled=True)  16.5 us
    psum x1, blocking collectives, on_device(): lax.psum((jnp.sum(query_wide * query_wide, axis=1), jnp.sum(key_wide * ke...  5.67 us

commit v1 on v0

v1 whole, which is shorter than its diff:
```python
import functools
import math

import jax
import jax.numpy as jnp
from jax import lax
from jax.experimental import pallas as pl
from jax.experimental.pallas import tpu as pltpu
from jax.sharding import PartitionSpec as P

EPSILON = 1e-06
NEG_FILL = -1e30
FRAME = 128
GROUP_FRAMES = 4
VMEM_BYTES = 60 * 1024 * 1024
V, K, G, Q = range(4)
MESH = pl.DeviceIdType.MESH


def dot(a, b, contract):
    return lax.dot_general(
        a, b, (contract, ((), ())), preferred_element_type=jnp.float32
    )


def nt(a, b):
    return dot(a, b, ((1,), (1,)))


def tn(a, b):
    return dot(a, b, ((0,), (0,)))


def nn(a, b):
    return dot(a, b, ((1,), (0,)))


def kernel(
    n_sec, n,
    q_hbm, k_hbm, v_hbm, g_hbm, q_gain_hbm, k_gain_hbm, stretch_hbm,
    att_hbm, dq_hbm, dk_hbm, dv_hbm,
    q_raw, k_raw, q_gain, k_gain, stretch, vb, kb, gb, qb, partner_stretch, sec, stats, s_buf, dp_buf,
    top, total, acc, dk_acc, dv_acc, att_out, dq_out, dk_out,
    recv, send_z, send_p, stretch_sem, sec_send, sec_recv, stat_send, stat_recv, local,
):
    rows, d = q_raw.shape
    span = 2
    levels = n // span
    width = d * n_sec
    scale = 1.0 / math.sqrt(d)
    log2_scale = scale * math.log2(math.e)
    me = lax.axis_index("seq")
    my_sec = lax.axis_index("section")
    level = me // span
    side = me % span
    partner = me + 1 - 2 * side
    has_up = level < levels - 1
    has_down = level > 0
    bufs = [vb, kb, gb, qb]

    loads = [
        pltpu.make_async_copy(q_hbm, q_raw, local.at[0]),
        pltpu.make_async_copy(k_hbm, k_raw, local.at[1]),
        pltpu.make_async_copy(v_hbm, vb.at[me], local.at[2]),
        pltpu.make_async_copy(g_hbm, gb.at[me], local.at[3]),
        pltpu.make_async_copy(q_gain_hbm, q_gain, local.at[4]),
        pltpu.make_async_copy(k_gain_hbm, k_gain, local.at[5]),
        pltpu.make_async_copy(stretch_hbm, stretch, local.at[6]),
    ]
    for load in loads:
        load.start()

    barrier = pltpu.get_barrier_semaphore()
    for step in range(1, n_sec):
        pl.semaphore_signal(
            barrier, inc=1, device_id={"section": lax.rem(my_sec + step, n_sec)},
            device_id_type=MESH,
        )
    for step in range(1, n):
        pl.semaphore_signal(
            barrier, inc=1, device_id={"seq": lax.rem(me + step, n)}, device_id_type=MESH
        )

    def remote(src, dst, send_sem, recv_sem, device):
        return pltpu.make_async_remote_copy(
            src_ref=src, dst_ref=dst, send_sem=send_sem, recv_sem=recv_sem,
            device_id=device, device_id_type=MESH,
        )

    def z_copy(a, slot, src=None):
        to = me + span if a in (V, K) else me - span
        block = bufs[a].at[slot]
        return remote(
            block if src is None else src, block, send_z.at[a, slot], recv.at[a, slot],
            {"seq": to},
        )

    def p_copy(a, slot, src=None):
        block = bufs[a].at[slot]
        return remote(
            block if src is None else src, block, send_p.at[a, slot], recv.at[a, slot],
            {"seq": partner},
        )

    def onward(a):
        return has_up if a in (V, K) else has_down

    def sec_copy(phase, step):
        return remote(
            sec.at[phase, 0], sec.at[phase, step], sec_send.at[phase, step],
            sec_recv.at[phase, step],
            {"section": lax.rem(my_sec + step, n_sec)},
        )

    def sec_start(phase):
        for step in range(1, n_sec):
            sec_copy(phase, step).start()

    def sec_sum(phase):
        result = sec[phase, 0]
        for step in range(1, n_sec):
            sec_copy(phase, step).wait_recv()
            result = result + sec[phase, step]
        return result

    def row_sum_of(matrix):
        return jnp.sum(matrix.T, axis=0, keepdims=True)

    def as_column(row):
        return jnp.broadcast_to(row, (d, rows)).T

    loads[0].wait()
    loads[1].wait()
    q_wide = q_raw[...].astype(jnp.float32)
    k_wide = k_raw[...].astype(jnp.float32)
    sec[0, 0] = jnp.zeros((8, rows), jnp.float32)
    sec[0, 0, 0:1, :] = row_sum_of(q_wide * q_wide)
    sec[0, 0, 1:2, :] = row_sum_of(k_wide * k_wide)

    pl.semaphore_wait(barrier, n_sec - 1 + n - 1)

    sec_start(0)
    for load in loads[4:]:
        load.wait()
    stretch_copy = remote(
        stretch, partner_stretch, stretch_sem.at[0], stretch_sem.at[1], {"seq": partner}
    )
    stretch_copy.start()
    for a, src in ((V, v_hbm), (G, g_hbm)):
        @pl.when(onward(a))
        def _():
            z_copy(a, me, src).start()
    for a, src in ((V, v_hbm), (G, g_hbm)):
        p_copy(a, me, src).start()

    squares = sec_sum(0)
    root = lax.rsqrt(squares * (1.0 / width) + EPSILON)
    q_root, k_root = root[0:1], root[1:2]
    kb[me] = (k_wide * as_column(k_root) * k_gain[...]).astype(jnp.bfloat16)
    @pl.when(has_up)
    def _():
        z_copy(K, me).start()
    p_copy(K, me).start()
    qb[me] = (q_wide * as_column(q_root) * q_gain[...]).astype(jnp.bfloat16)
    @pl.when(has_down)
    def _():
        z_copy(Q, me).start()
    p_copy(Q, me).start()
    loads[2].wait()
    loads[3].wait()

    def hidden_bias(key_stretch, query_stretch):
        parts = []
        for at in range(0, rows, FRAME):
            row = jnp.where(key_stretch[:, at : at + 1] <= query_stretch, 0.0, NEG_FILL)
            parts.append(jnp.broadcast_to(row, (FRAME, rows)))
        return jnp.concatenate(parts, axis=0)

    top[...] = jnp.full((1, rows), NEG_FILL, jnp.float32)
    total[...] = jnp.zeros((1, rows), jnp.float32)
    acc[...] = jnp.zeros_like(acc)

    def forward(b, bias=None):
        scores = nt(kb[b], qb[me]) * log2_scale
        if bias is not None:
            scores = scores + bias
        s_buf[b] = scores
        old = top[...]
        new = jnp.maximum(old, jnp.max(scores, axis=0, keepdims=True))
        weights = jnp.exp2(scores - new)
        factor = jnp.exp2(old - new)
        top[...] = new
        total[...] = total[...] * factor + jnp.sum(weights, axis=0, keepdims=True)
        acc[...] = acc[...] * factor + tn(vb[b], weights.astype(jnp.bfloat16))
        dp_buf[b] = nt(vb[b], gb[me])

    def key_scores(b, slot, bias=None):
        scores = nt(kb[me], qb[b]) * log2_scale
        if bias is not None:
            scores = scores + bias
        s_buf[slot] = scores
        dp_buf[slot] = nt(vb[me], gb[b])

    own_stretch = stretch[...]
    forward(me, hidden_bias(own_stretch, own_stretch))

    def stat_copy(b, slot):
        return remote(
            stats.at[slot], stats.at[slot], stat_send.at[b], stat_recv.at[slot], {"seq": b}
        )

    def loop(start, stop, body):
        def run(i, carry):
            body(i)
            return carry
        lax.fori_loop(start, stop, run, 0)

    att_store = pltpu.make_async_copy(att_out, att_hbm, local.at[0])

    def finish_forward():
        attended = (acc[...] / total[...]).astype(jnp.bfloat16).astype(jnp.float32)
        log_total = top[...] + jnp.log2(total[...])
        delta = jnp.sum(gb[me].astype(jnp.float32).T * attended, axis=0, keepdims=True)
        stats[me] = jnp.zeros((8, rows), jnp.float32)
        stats[me, 0:1, :] = log_total
        stats[me, 1:2, :] = delta

        def stat_start(b):
            @pl.when(b != me)
            def _():
                stat_copy(b, me).start()

        loop(0, (level + 1) * span, stat_start)
        att_out[...] = attended.T.astype(jnp.bfloat16)
        att_store.start()
        acc[...] = jnp.zeros_like(acc)

        def query_tail(at):
            pair = pl.ds(at * span, span)
            scores = s_buf[pair].reshape(span * rows, rows)
            chances = jnp.exp2(scores - log_total)
            grads = chances * (dp_buf[pair].reshape(span * rows, rows) - delta)
            acc[...] += tn(kb[pair].reshape(span * rows, d), grads.astype(jnp.bfloat16))

        loop(0, level + 1, query_tail)
        dq = acc[...].T * scale
        dq_out[...] = dq
        sec[1, 0] = jnp.broadcast_to(
            row_sum_of(dq * q_gain[...] * q_raw[...].astype(jnp.float32)), (8, rows)
        )
        sec_start(1)

    dk_acc[...] = jnp.zeros_like(dk_acc)
    dv_acc[...] = jnp.zeros_like(dv_acc)

    def key_level(at):
        key_grad, value_grad = [], []
        for r in range(span):
            b = at * span + r
            @pl.when(b != me)
            def _():
                stat_copy(partner, b).wait_recv()
        for r in range(span):
            b = at * span + r
            slot = jnp.where(b == partner, n, b)
            chances = jnp.exp2(s_buf[slot] - stats[b, 0:1, :])
            value_grad.append(nn(chances.astype(jnp.bfloat16), gb[b]))
            grads = chances * (dp_buf[slot] - stats[b, 1:2, :])
            key_grad.append(nn(grads.astype(jnp.bfloat16), qb[b]))
        dv_acc[...] += sum(value_grad)
        dk_acc[...] += sum(key_grad)

    def step(s, first):
        low, high = me - span * s, me + span * s
        for a in (V, G, K, Q):
            slot = low if a in (V, K) else high
            @pl.when(low >= 0 if a in (V, K) else high < n)
            def _():
                p_copy(a, slot).wait_recv()
                @pl.when(onward(a))
                def _():
                    z_copy(a, slot).start()
                if not first:
                    p_copy(a, slot).start()
        if first:
            for a in (V, G, K, Q):
                p_copy(a, partner).wait_recv()
                @pl.when(onward(a))
                def _():
                    z_copy(a, partner).start()
            stretch_copy.wait_recv()
            other_stretch = partner_stretch[...]
            forward(partner, hidden_bias(other_stretch, own_stretch))
            @pl.when(level == 0)
            def _():
                finish_forward()
            key_scores(partner, n, hidden_bias(own_stretch, other_stretch))
        @pl.when(low >= 0)
        def _():
            forward(low)
        @pl.when(high < n)
        def _():
            key_scores(high, high)
        if not first:
            across(s - 1)
            @pl.when(level == s - 1)
            def _():
                finish_forward()
            @pl.when(level <= s - 2)
            def _():
                key_level(s - 2)

    def across(s):
        low, high = partner - span * s, partner + span * s
        @pl.when(low >= 0)
        def _():
            p_copy(V, low).wait_recv()
            p_copy(K, low).wait_recv()
            forward(low)
        @pl.when(high < n)
        def _():
            p_copy(G, high).wait_recv()
            p_copy(Q, high).wait_recv()
            key_scores(high, high)

    step(1, True)
    loop(2, levels, lambda s: step(s, False))
    across(levels - 1)
    @pl.when(level == levels - 1)
    def _():
        finish_forward()

    loop(jnp.maximum(level, levels - 2), levels, key_level)
    dv_store = pltpu.make_async_copy(dv_acc, dv_hbm, local.at[1])
    dv_store.start()
    dk = dk_acc[...] * scale
    sec[2, 0] = jnp.broadcast_to(row_sum_of(dk * k_gain[...] * k_wide), (8, rows))
    sec_start(2)

    q_part = q_root * q_root * q_root * (sec_sum(1)[0:1] * (1.0 / width))
    dq_out[...] = q_gain[...] * as_column(q_root) * dq_out[...] - q_wide * as_column(q_part)
    dq_store = pltpu.make_async_copy(dq_out, dq_hbm, local.at[2])
    dq_store.start()
    k_part = k_root * k_root * k_root * (sec_sum(2)[0:1] * (1.0 / width))
    dk_out[...] = k_gain[...] * as_column(k_root) * dk - k_wide * as_column(k_part)
    dk_store = pltpu.make_async_copy(dk_out, dk_hbm, local.at[3])
    dk_store.start()

    for phase in range(3):
        for s in range(1, n_sec):
            sec_copy(phase, s).wait_send()
    stretch_copy.wait_send()

    def stat_end(b):
        @pl.when(b != me)
        def _():
            stat_copy(b, me).wait_send()

    loop(0, (level + 1) * span, stat_end)
    for a in range(4):
        p_copy(a, me).wait_send()
        @pl.when(onward(a))
        def _():
            z_copy(a, me).wait_send()
            z_copy(a, partner).wait_send()

        def sent(s):
            slot = me - span * s if a in (V, K) else me + span * s
            @pl.when(slot >= 0 if a in (V, K) else slot < n)
            def _():
                @pl.when(onward(a))
                def _():
                    z_copy(a, slot).wait_send()
                @pl.when(s >= 2)
                def _():
                    p_copy(a, slot).wait_send()

        loop(1, levels, sent)
    att_store.wait()
    dv_store.wait()
    dq_store.wait()
    dk_store.wait()


def store_kernel(*refs):
    sources, targets, sems = refs[:4], refs[4:8], refs[8]
    copies = [
        pltpu.make_async_copy(source, target, sems.at[i])
        for i, (source, target) in enumerate(zip(sources, targets))
    ]
    for copy in copies:
        copy.start()
    for copy in copies:
        copy.wait()


def on_device(n_sec, n, queries, key_rows, values, out_grad, query_gain, key_gain, stretch_id):
    rows, d = queries.shape
    assert rows * 2 == FRAME * GROUP_FRAMES and n % 2 == 0
    f32, bf16 = jnp.float32, jnp.bfloat16
    any_space = pl.BlockSpec(memory_space=pl.ANY)
    hbm = pl.BlockSpec(memory_space=pltpu.HBM)
    dma = pltpu.SemaphoreType.DMA
    block = pltpu.VMEM((n, rows, d), bf16)
    shapes = (jax.ShapeDtypeStruct((rows, d), bf16),) + (jax.ShapeDtypeStruct((rows, d), f32),) * 3
    results = pl.pallas_call(
        functools.partial(kernel, n_sec, n),
        out_shape=shapes,
        in_specs=[hbm] * 7,
        out_specs=(any_space,) * 4,
        scratch_shapes=[
            pltpu.VMEM((rows, d), bf16),
            pltpu.VMEM((rows, d), bf16),
            pltpu.VMEM((1, d), f32),
            pltpu.VMEM((1, d), f32),
            pltpu.VMEM((1, rows), jnp.int32),
            block, block, block, block,
            pltpu.VMEM((1, rows), jnp.int32),
            pltpu.VMEM((3, n_sec, 8, rows), f32),
            pltpu.VMEM((n, 8, rows), f32),
            pltpu.VMEM((n + 1, rows, rows), f32),
            pltpu.VMEM((n + 1, rows, rows), f32),
            pltpu.VMEM((1, rows), f32),
            pltpu.VMEM((1, rows), f32),
            pltpu.VMEM((d, rows), f32),
            pltpu.VMEM((rows, d), f32),
            pltpu.VMEM((rows, d), f32),
            pltpu.VMEM((rows, d), bf16),
            pltpu.VMEM((rows, d), f32),
            pltpu.VMEM((rows, d), f32),
            dma((4, n)),
            dma((4, n)),
            dma((4, n)),
            dma((2,)),
            dma((3, n_sec)),
            dma((3, n_sec)),
            dma((n,)),
            dma((n,)),
            dma((7,)),
        ],
        compiler_params=pltpu.CompilerParams(
            collective_id=0, has_side_effects=True, vmem_limit_bytes=VMEM_BYTES
        ),
        name="stretch_attention",
    )(
        queries, key_rows, values, out_grad,
        query_gain.reshape(1, d), key_gain.reshape(1, d), stretch_id.reshape(1, rows),
    )
    return pl.pallas_call(
        store_kernel,
        out_shape=shapes,
        in_specs=[any_space] * 4,
        out_specs=(hbm,) * 4,
        scratch_shapes=[dma((4,))],
        compiler_params=pltpu.CompilerParams(vmem_limit_bytes=VMEM_BYTES),
        name="store_results",
    )(*results)


def solution(mesh):
    placed = (
        P("seq", "section"),
        P("seq", "section"),
        P("seq", "section"),
        P("seq", "section"),
        P("section"),
        P("section"),
        P("seq"),
    )
    return jax.shard_map(
        functools.partial(on_device, mesh.shape["section"], mesh.shape["seq"]),
        mesh=mesh,
        in_specs=placed,
        out_specs=(P("seq", "section"),) * 4,
        check_vma=False,
    )
```

time: 209 us -> 49 us (0.23)
  blocking collectives: 194 us -> 0 us
  Pallas kernels: 0 us -> 48.2 us
  matrix products: 6.14 us -> 0 us
  other arithmetic: 4.48 us -> 0 us
  local copies, waits for them, and re-layouts: 2.85 us -> 0 us
    all_gather x7 -> x0, blocking collectives: 182 us -> none  [the longest x1 31.5 us: on_device(): lax.all_gather(key_hat, 'seq', axis=0, tiled=True)]
    pallas_call x0 -> x2, Pallas kernels: none -> 48.2 us  [the longest x1 33.2 us: on_device(): pl.pallas_call(functools.partial(kernel, n_sec, n), out_shape=shapes, in_...]
    psum x2 -> x0, blocking collectives: 11.3 us -> none  [the longest x1 5.67 us: on_device(): lax.psum((jnp.sum(query_wide * query_wide, axis=1), jnp.sum(key_wide * ke...]
    dot_general x14 -> x0, matrix products: 6.14 us -> none  [the longest x2 1.38 us: key_side_update(): jnp.einsum('tu,td->ud', grad_scores, query_part, preferred_element_type=j...]
    unnamed x16 -> x0, local copies, waits for them, and re-layouts: 2.73 us -> none
    reduce_sum x7 -> x0, other arithmetic: 2.54 us -> none  [the longest x1 1.01 us: on_device(): jnp.sum(key_wide * key_wide, axis=1)]
where the time goes in v1:
time: 49 us; the launch traced here: 48.9 us
  Pallas kernels  48.2 us (98%)
  between operations  0.64 us (1%)
    pallas_call x1, Pallas kernels, on_device(): pl.pallas_call(functools.partial(kernel, n_sec, n), out_shape=shapes, in_...  33.2 us
    pallas_call x1, Pallas kernels, on_device(): pl.pallas_call(store_kernel, out_shape=shapes, in_specs=[any_space] * 4,...  15 us

profile of v1, /device:TPU:0, one launch (start us, length us, event | category | flops | bytes accessed | tf_op | source)
XLA Modules:
  0.0 48.9 jit_solution(13845201256118508403)
XLA Ops:
  0.6 33.2 %stretch_attention.1 = (bf16[256,128]{1,0:T(8,128)(2,1)}, f32[256,128]{1,0:T(8,128)}, f32[256,128]{1,0:T(8,128)}, f32[256,128]{1,0:T(8,128)}) custom-call(bf16[256,128]{1,0:T(8,128)(2,1)} %q_hbm.1, bf16[256,128]{1,0:T(8,128)(2,1)} %k_hbm.1, bf16[256,128]{1,0:T(8,128)(2,1)} %v_hbm.1, bf16[256,128]{1,0:T(8,128)(2,1)} %g_hbm.1, f32[1,128]{1,0:T(1,128)} %bitcast.4, ...), custom_call_target="tpu_custom_call" | custom-call | tf_op jit(solution)/shard_map/stretch_attention/pallas_call | solution.py:406
  33.8 15.0 %store_results.1 = (bf16[256,128]{1,0:T(8,128)(2,1)}, f32[256,128]{1,0:T(8,128)}, f32[256,128]{1,0:T(8,128)}, f32[256,128]{1,0:T(8,128)}) custom-call(bf16[256,128]{1,0:T(8,128)(2,1)} %get-tuple-element.8.refs_0_, f32[256,128]{1,0:T(8,128)} %get-tuple-element.9.refs_1_, f32[256,128]{1,0:T(8,128)} %get-tuple-element.10.refs_2_, ...), custom_call_target="tpu_custom_call" | custom-call | tf_op jit(solution)/shard_map/store_results/pallas_call | solution.py:449

commit v2 on v1

--- a/solution.py
+++ b/solution.py
@@ -192,7 +192,6 @@
         top[...] = new
         total[...] = total[...] * factor + jnp.sum(weights, axis=0, keepdims=True)
         acc[...] = acc[...] * factor + tn(vb[b], weights.astype(jnp.bfloat16))
-        dp_buf[b] = nt(vb[b], gb[me])
 
     def key_scores(b, slot, bias=None):
         scores = nt(kb[me], qb[b]) * log2_scale
@@ -203,6 +202,7 @@
 
     own_stretch = stretch[...]
     forward(me, hidden_bias(own_stretch, own_stretch))
+    dp_buf[me] = nt(vb[me], gb[me])
 
     def stat_copy(b, slot):
         return remote(
@@ -233,13 +233,16 @@
         loop(0, (level + 1) * span, stat_start)
         att_out[...] = attended.T.astype(jnp.bfloat16)
         att_store.start()
+
+    def query_side():
         acc[...] = jnp.zeros_like(acc)
+        log_total, delta = stats[me, 0:1, :], stats[me, 1:2, :]
 
         def query_tail(at):
             pair = pl.ds(at * span, span)
             scores = s_buf[pair].reshape(span * rows, rows)
             chances = jnp.exp2(scores - log_total)
-            grads = chances * (dp_buf[pair].reshape(span * rows, rows) - delta)
+            grads = chances * (nt(vb[pair].reshape(span * rows, d), gb[me]) - delta)
             acc[...] += tn(kb[pair].reshape(span * rows, d), grads.astype(jnp.bfloat16))
 
         loop(0, level + 1, query_tail)
@@ -294,11 +297,12 @@
             @pl.when(level == 0)
             def _():
                 finish_forward()
-            key_scores(partner, n, hidden_bias(own_stretch, other_stretch))
+                query_side()
+                key_scores(partner, n, hidden_bias(own_stretch, other_stretch))
         @pl.when(low >= 0)
         def _():
             forward(low)
-        @pl.when(high < n)
+        @pl.when((high < n) & (level == 0))
         def _():
             key_scores(high, high)
         if not first:
@@ -306,7 +310,7 @@
             @pl.when(level == s - 1)
             def _():
                 finish_forward()
-            @pl.when(level <= s - 2)
+            @pl.when((level == 0) & (s >= 2))
             def _():
                 key_level(s - 2)
 
@@ -321,7 +325,9 @@
         def _():
             p_copy(G, high).wait_recv()
             p_copy(Q, high).wait_recv()
-            key_scores(high, high)
+            @pl.when(level == 0)
+            def _():
+                key_scores(high, high)
 
     step(1, True)
     loop(2, levels, lambda s: step(s, False))
@@ -330,7 +336,18 @@
     def _():
         finish_forward()
 
-    loop(jnp.maximum(level, levels - 2), levels, key_level)
+    def key_scores_level(at):
+        for r in range(span):
+            key_scores(at * span + r, at * span + r)
+
+    @pl.when(level > 0)
+    def _():
+        query_side()
+        other_stretch = partner_stretch[...]
+        key_scores(partner, n, hidden_bias(own_stretch, other_stretch))
+        loop(level + 1, levels, key_scores_level)
+
+    loop(jnp.where(level == 0, levels - 2, level), levels, key_level)
     dv_store = pltpu.make_async_copy(dv_acc, dv_hbm, local.at[1])
     dv_store.start()
     dk = dk_acc[...] * scale
@@ -383,15 +400,16 @@
 
 
 def store_kernel(*refs):
-    sources, targets, sems = refs[:4], refs[4:8], refs[8]
-    copies = [
-        pltpu.make_async_copy(source, target, sems.at[i])
-        for i, (source, target) in enumerate(zip(sources, targets))
-    ]
-    for copy in copies:
-        copy.start()
-    for copy in copies:
-        copy.wait()
+    sources, targets, staged, sems = refs[:4], refs[4:8], refs[8:12], refs[12]
+    loads = [pltpu.make_async_copy(sources[i], staged[i], sems.at[0, i]) for i in range(4)]
+    stores = [pltpu.make_async_copy(staged[i], targets[i], sems.at[1, i]) for i in range(4)]
+    for load in loads:
+        load.start()
+    for load, store in zip(loads, stores):
+        load.wait()
+        store.start()
+    for store in stores:
+        store.wait()
 
 
 def on_device(n_sec, n, queries, key_rows, values, out_grad, query_gain, key_gain, stretch_id):
@@ -451,7 +469,7 @@
         out_shape=shapes,
         in_specs=[any_space] * 4,
         out_specs=(hbm,) * 4,
-        scratch_shapes=[dma((4,))],
+        scratch_shapes=[pltpu.VMEM(shape.shape, shape.dtype) for shape in shapes] + [dma((2, 4))],
         compiler_params=pltpu.CompilerParams(vmem_limit_bytes=VMEM_BYTES),
         name="store_results",
     )(*results)

time: 49 us -> 35.9 us (0.73)
  Pallas kernels: 48.2 us -> 35 us
    pallas_call x1, Pallas kernels: 15 us -> 1.79 us  [on_device(): pl.pallas_call(store_kernel, out_shape=shapes, in_specs=[any_space] * 4,...]
where the time goes in v2:
time: 35.9 us; the launch traced here: 35.7 us
  Pallas kernels  35 us (97%)
  between operations  0.64 us (2%)
    pallas_call x1, Pallas kernels, on_device(): pl.pallas_call(functools.partial(kernel, n_sec, n), out_shape=shapes, in_...  33.2 us
    pallas_call x1, Pallas kernels, on_device(): pl.pallas_call(store_kernel, out_shape=shapes, in_specs=[any_space] * 4,...  1.79 us

profile of v2, /device:TPU:0, one launch (start us, length us, event | category | flops | bytes accessed | tf_op | source)
XLA Modules:
  0.0 35.7 jit_solution(16103218402990301434)
XLA Ops:
  0.6 33.2 %stretch_attention.1 = (bf16[256,128]{1,0:T(8,128)(2,1)}, f32[256,128]{1,0:T(8,128)}, f32[256,128]{1,0:T(8,128)}, f32[256,128]{1,0:T(8,128)}) custom-call(bf16[256,128]{1,0:T(8,128)(2,1)} %q_hbm.1, bf16[256,128]{1,0:T(8,128)(2,1)} %k_hbm.1, bf16[256,128]{1,0:T(8,128)(2,1)} %v_hbm.1, bf16[256,128]{1,0:T(8,128)(2,1)} %g_hbm.1, f32[1,128]{1,0:T(1,128)} %bitcast.4, ...), custom_call_target="tpu_custom_call" | custom-call | tf_op jit(solution)/shard_map/stretch_attention/pallas_call | solution.py:424
  33.9 1.8 %store_results.1 = (bf16[256,128]{1,0:T(8,128)(2,1)}, f32[256,128]{1,0:T(8,128)}, f32[256,128]{1,0:T(8,128)}, f32[256,128]{1,0:T(8,128)}) custom-call(bf16[256,128]{1,0:T(8,128)(2,1)} %get-tuple-element.8.refs_0_, f32[256,128]{1,0:T(8,128)} %get-tuple-element.9.refs_1_, f32[256,128]{1,0:T(8,128)} %get-tuple-element.10.refs_2_, ...), custom_call_target="tpu_custom_call" | custom-call | tf_op jit(solution)/shard_map/store_results/pallas_call | solution.py:467

commit v3 on v2

--- a/solution.py
+++ b/solution.py
@@ -285,12 +285,17 @@
                     z_copy(a, slot).start()
                 if not first:
                     p_copy(a, slot).start()
+            if not first:
+                @pl.when((s == 2) & onward(a))
+                def _():
+                    z_copy(a, partner).start()
         if first:
             for a in (V, G, K, Q):
                 p_copy(a, partner).wait_recv()
-                @pl.when(onward(a))
-                def _():
-                    z_copy(a, partner).start()
+                if levels == 2:
+                    @pl.when(onward(a))
+                    def _():
+                        z_copy(a, partner).start()
             stretch_copy.wait_recv()
             other_stretch = partner_stretch[...]
             forward(partner, hidden_bias(other_stretch, own_stretch))

time: 35.9 us -> 38.2 us (1.064)
  Pallas kernels: 35 us -> 37.4 us
    pallas_call x1, Pallas kernels: 33.2 us -> 35.6 us  [on_device(): pl.pallas_call(functools.partial(kernel, n_sec, n), out_shape=shapes, in_...]
where the time goes in v3:
time: 38.2 us; the launch traced here: 38 us
  Pallas kernels  37.4 us (98%)
  between operations  0.64 us (2%)
    pallas_call x1, Pallas kernels, on_device(): pl.pallas_call(functools.partial(kernel, n_sec, n), out_shape=shapes, in_...  35.6 us
    pallas_call x1, Pallas kernels, on_device(): pl.pallas_call(store_kernel, out_shape=shapes, in_specs=[any_space] * 4,...  1.79 us

profile of v3, /device:TPU:0, one launch (start us, length us, event | category | flops | bytes accessed | tf_op | source)
XLA Modules:
  0.0 38.0 jit_solution(10631163728288264630)
XLA Ops:
  0.6 35.6 %stretch_attention.1 = (bf16[256,128]{1,0:T(8,128)(2,1)}, f32[256,128]{1,0:T(8,128)}, f32[256,128]{1,0:T(8,128)}, f32[256,128]{1,0:T(8,128)}) custom-call(bf16[256,128]{1,0:T(8,128)(2,1)} %q_hbm.1, bf16[256,128]{1,0:T(8,128)(2,1)} %k_hbm.1, bf16[256,128]{1,0:T(8,128)(2,1)} %v_hbm.1, bf16[256,128]{1,0:T(8,128)(2,1)} %g_hbm.1, f32[1,128]{1,0:T(1,128)} %bitcast.4, ...), custom_call_target="tpu_custom_call" | custom-call | tf_op jit(solution)/shard_map/stretch_attention/pallas_call | solution.py:429
  36.2 1.8 %store_results.1 = (bf16[256,128]{1,0:T(8,128)(2,1)}, f32[256,128]{1,0:T(8,128)}, f32[256,128]{1,0:T(8,128)}, f32[256,128]{1,0:T(8,128)}) custom-call(bf16[256,128]{1,0:T(8,128)(2,1)} %get-tuple-element.8.refs_0_, f32[256,128]{1,0:T(8,128)} %get-tuple-element.9.refs_1_, f32[256,128]{1,0:T(8,128)} %get-tuple-element.10.refs_2_, ...), custom_call_target="tpu_custom_call" | custom-call | tf_op jit(solution)/shard_map/store_results/pallas_call | solution.py:472

commit v4 on v2

--- a/solution.py
+++ b/solution.py
@@ -12,6 +12,7 @@
 NEG_FILL = -1e30
 FRAME = 128
 GROUP_FRAMES = 4
+FAR = 3
 VMEM_BYTES = 60 * 1024 * 1024
 V, K, G, Q = range(4)
 MESH = pl.DeviceIdType.MESH
@@ -41,7 +42,7 @@
     att_hbm, dq_hbm, dk_hbm, dv_hbm,
     q_raw, k_raw, q_gain, k_gain, stretch, vb, kb, gb, qb, partner_stretch, sec, stats, s_buf, dp_buf,
     top, total, acc, dk_acc, dv_acc, att_out, dq_out, dk_out,
-    recv, send_z, send_p, stretch_sem, sec_send, sec_recv, stat_send, stat_recv, local,
+    recv, send_z, send_p, send_far, stretch_sem, sec_send, sec_recv, stat_send, stat_recv, local,
 ):
     rows, d = q_raw.shape
     span = 2
@@ -102,6 +103,16 @@
             {"seq": partner},
         )
 
+    def far_copy(a, src=None):
+        block = bufs[a].at[me]
+        to = me + FAR * span if a in (V, K) else me - FAR * span
+        return remote(
+            block if src is None else src, block, send_far.at[a], recv.at[a, me], {"seq": to}
+        )
+
+    def far(a):
+        return level + FAR < levels if a in (V, K) else level >= FAR
+
     def onward(a):
         return has_up if a in (V, K) else has_down
 
@@ -147,6 +158,9 @@
     )
     stretch_copy.start()
     for a, src in ((V, v_hbm), (G, g_hbm)):
+        @pl.when(far(a))
+        def _():
+            far_copy(a, src).start()
         @pl.when(onward(a))
         def _():
             z_copy(a, me, src).start()
@@ -157,11 +171,17 @@
     root = lax.rsqrt(squares * (1.0 / width) + EPSILON)
     q_root, k_root = root[0:1], root[1:2]
     kb[me] = (k_wide * as_column(k_root) * k_gain[...]).astype(jnp.bfloat16)
+    @pl.when(far(K))
+    def _():
+        far_copy(K).start()
     @pl.when(has_up)
     def _():
         z_copy(K, me).start()
     p_copy(K, me).start()
     qb[me] = (q_wide * as_column(q_root) * q_gain[...]).astype(jnp.bfloat16)
+    @pl.when(far(Q))
+    def _():
+        far_copy(Q).start()
     @pl.when(has_down)
     def _():
         z_copy(Q, me).start()
@@ -273,14 +293,26 @@
         dv_acc[...] += sum(value_grad)
         dk_acc[...] += sum(key_grad)
 
-    def step(s, first):
+    def distance(i):
+        if levels <= FAR:
+            return i
+        return jnp.where(i == FAR - 1, FAR, jnp.where(i == FAR, FAR - 1, i))
+
+    def finished_at(i):
+        if levels <= FAR:
+            return level == i
+        late = (i == FAR) & (level == FAR - 1)
+        return ((i != FAR - 1) & (level == i)) | late
+
+    def step(i, first):
+        s = 1 if first else distance(i)
         low, high = me - span * s, me + span * s
         for a in (V, G, K, Q):
             slot = low if a in (V, K) else high
             @pl.when(low >= 0 if a in (V, K) else high < n)
             def _():
                 p_copy(a, slot).wait_recv()
-                @pl.when(onward(a))
+                @pl.when(onward(a) & (s != FAR - 1))
                 def _():
                     z_copy(a, slot).start()
                 if not first:
@@ -306,13 +338,13 @@
         def _():
             key_scores(high, high)
         if not first:
-            across(s - 1)
-            @pl.when(level == s - 1)
+            across(distance(i - 1))
+            @pl.when(finished_at(i - 1))
             def _():
                 finish_forward()
-            @pl.when((level == 0) & (s >= 2))
-            def _():
-                key_level(s - 2)
+            @pl.when(level == 0)
+            def _():
+                key_level(i - 2)
 
     def across(s):
         low, high = partner - span * s, partner + span * s
@@ -330,9 +362,9 @@
                 key_scores(high, high)
 
     step(1, True)
-    loop(2, levels, lambda s: step(s, False))
-    across(levels - 1)
-    @pl.when(level == levels - 1)
+    loop(2, levels, lambda i: step(i, False))
+    across(distance(levels - 1))
+    @pl.when(finished_at(levels - 1))
     def _():
         finish_forward()
 
@@ -380,12 +412,15 @@
         def _():
             z_copy(a, me).wait_send()
             z_copy(a, partner).wait_send()
+        @pl.when(far(a))
+        def _():
+            far_copy(a).wait_send()
 
         def sent(s):
             slot = me - span * s if a in (V, K) else me + span * s
             @pl.when(slot >= 0 if a in (V, K) else slot < n)
             def _():
-                @pl.when(onward(a))
+                @pl.when(onward(a) & (s != FAR - 1))
                 def _():
                     z_copy(a, slot).wait_send()
                 @pl.when(s >= 2)
@@ -449,6 +484,7 @@
             dma((4, n)),
             dma((4, n)),
             dma((4, n)),
+            dma((4,)),
             dma((2,)),
             dma((3, n_sec)),
             dma((3, n_sec)),

time: 35.9 us -> 36.3 us (1.011)
  Pallas kernels: 35 us -> 35.5 us
    pallas_call x1, Pallas kernels: 33.2 us -> 33.7 us  [on_device(): pl.pallas_call(functools.partial(kernel, n_sec, n), out_shape=shapes, in_...]
where the time goes in v4:
time: 36.3 us; the launch traced here: 36.1 us
  Pallas kernels  35.5 us (98%)
  between operations  0.64 us (2%)
    pallas_call x1, Pallas kernels, on_device(): pl.pallas_call(functools.partial(kernel, n_sec, n), out_shape=shapes, in_...  33.7 us
    pallas_call x1, Pallas kernels, on_device(): pl.pallas_call(store_kernel, out_shape=shapes, in_specs=[any_space] * 4,...  1.79 us

profile of v4, /device:TPU:0, one launch (start us, length us, event | category | flops | bytes accessed | tf_op | source)
XLA Modules:
  0.0 36.1 jit_solution(396127161589437460)
XLA Ops:
  0.6 33.7 %stretch_attention.1 = (bf16[256,128]{1,0:T(8,128)(2,1)}, f32[256,128]{1,0:T(8,128)}, f32[256,128]{1,0:T(8,128)}, f32[256,128]{1,0:T(8,128)}) custom-call(bf16[256,128]{1,0:T(8,128)(2,1)} %q_hbm.1, bf16[256,128]{1,0:T(8,128)(2,1)} %k_hbm.1, bf16[256,128]{1,0:T(8,128)(2,1)} %v_hbm.1, bf16[256,128]{1,0:T(8,128)(2,1)} %g_hbm.1, f32[1,128]{1,0:T(1,128)} %bitcast.4, ...), custom_call_target="tpu_custom_call" | custom-call | tf_op jit(solution)/shard_map/stretch_attention/pallas_call | solution.py:459
  34.4 1.8 %store_results.1 = (bf16[256,128]{1,0:T(8,128)(2,1)}, f32[256,128]{1,0:T(8,128)}, f32[256,128]{1,0:T(8,128)}, f32[256,128]{1,0:T(8,128)}) custom-call(bf16[256,128]{1,0:T(8,128)(2,1)} %get-tuple-element.8.refs_0_, f32[256,128]{1,0:T(8,128)} %get-tuple-element.9.refs_1_, f32[256,128]{1,0:T(8,128)} %get-tuple-element.10.refs_2_, ...), custom_call_target="tpu_custom_call" | custom-call | tf_op jit(solution)/shard_map/store_results/pallas_call | solution.py:503
